TPU v7x, 32 devices: a whole 2x2x4 slice. The times are simulated.
32 devices in a mesh: dp: 8 (over z, x), tensor: 4 (over y, core).
Axes of the slice: x: 2, y: 2, z: 4, core: 2. Of those that a mesh axis runs over, the one named last changes fastest.
Arguments:
- grads: bfloat16 [8, 3072, 8192], P('dp', None, 'tensor'), may hold values from -8 to 8
- errors: bfloat16 [8, 3072, 8192], P('dp', None, 'tensor'), may hold values from -4 to 4
- q_init: float32 [8192, 32], P('tensor'), may hold values from -0.0625 to 0.0625
Outputs:
- left_sum: float32 [3072, 32], P(('dp', 'tensor'))
- right: float32 [8192, 32], P('tensor')
- new_errors: bfloat16 [8, 3072, 8192], P('dp', None, 'tensor')
All inputs are finite; a program needn't handle non-finite values.
Results may differ from a plain program's by a relative error of at most 0.0085.
Values sent between devices are 32-bit elements; how exact they have to be, the bound alone decides.
A program may use at most 128 MiB of HBM per device.

v0:
```python
import jax
import jax.numpy as jnp
from jax import lax
from jax.sharding import PartitionSpec as P


def on_device(grads, errors, q_init):
    replicas = lax.axis_size("dp")
    merged = (grads[0].astype(jnp.float32) + errors[0].astype(jnp.float32)).astype(jnp.bfloat16)
    q_low = q_init.astype(jnp.bfloat16)
    partial_left = jnp.dot(merged, q_low, preferred_element_type=jnp.float32)
    left_full = lax.psum(partial_left, ("dp", "tensor")) / replicas
    share_rows = merged.shape[0] // (replicas * lax.axis_size("tensor"))
    position = lax.axis_index(("dp", "tensor"))
    left_out = lax.dynamic_slice_in_dim(left_full, position * share_rows, share_rows, 0)
    gram = jnp.dot(left_full.T, left_full, precision=lax.Precision.HIGHEST)
    lower = jnp.linalg.cholesky(gram)
    basis = jax.scipy.linalg.solve_triangular(lower, left_full.T, lower=True).T
    basis_low = basis.astype(jnp.bfloat16)
    local_right = jnp.dot(merged.T, basis_low, preferred_element_type=jnp.float32)
    right = lax.psum(local_right, "dp") / replicas
    approx = jnp.dot(basis, right.T, precision=lax.Precision.HIGHEST)
    renewed = (merged.astype(jnp.float32) - approx).astype(jnp.bfloat16)
    return (left_out, right, renewed[None])


def solution(mesh):
    return jax.shard_map(
        on_device,
        mesh=mesh,
        in_specs=(P("dp", None, "tensor"), P("dp", None, "tensor"), P("tensor", None)),
        out_specs=(P(("dp", "tensor"), None), P("tensor", None), P("dp", None, "tensor")),
        check_vma=False,
    )
```

profile of v0, /device:TPU:0, one launch (start us, length us, event | category | flops | bytes accessed | tf_op | source)
XLA Modules:
  0.0 276.1 jit_solution(3430065236785520737)
XLA Ops:
  7.2 0.0 all-reduce.3.cloned.1.call-start
  7.2 12.8 %fusion.4 = f32[3072,32]{0,1:T(8,128)} fusion(f32[2048,32]{0,1:T(8,128)} %param.5, bf16[1,3072,2048]{2,1,0:T(8,128)(2,1)} %param.4, bf16[1,3072,2048]{2,1,0:T(8,128)(2,1)} %param.3), kind=kOutput, calls=%fused_computation.8 | convolution fusion | flops 427884544 | bytes 25821184 | tf_op jit(solution)/shard_map/dot_general | solution.py:11
  20.0 0.0 all-reduce.3.cloned.1.call-update
  20.0 0.2 all-reduce.5.cloned.1.call-start
  20.3 130.1 %all-reduce.3.cloned.1.call-done = f32[3072,32]{0,1:T(8,128)} async-done(((f32[3072,32]{0,1:T(8,128)}), f32[3072,32]{0,1:T(8,128)}) %all-reduce.3.cloned.1.call-update) | async-done | bytes 393232 | tf_op jit(solution)/shard_map/psum | solution.py:12
  150.4 1.6 fusion.10
  152.0 0.1 copy.6
  152.1 2.9 %cholesky.16 = f32[32,32]{1,0:T(8,128)S(1)} custom-call(f32[32,32]{1,0:T(8,128)S(1)} %fusion.9), custom_call_target="Cholesky" | custom-call | tf_op jit(solution)/shard_map/jit(cholesky)/cholesky | solution.py:17
  155.0 0.6 compare_reduce_fusion
  155.7 0.7 fusion.6
  156.3 2.4 custom-call.7
  158.8 1.5 fusion.7
  160.3 0.0 copy-start
  160.3 10.7 %fusion.2 = f32[2048,32]{0,1:T(8,128)} fusion(f32[32,3072]{1,0:T(8,128)S(1)} %fusion.7, bf16[1,3072,2048]{2,1,0:T(8,128)(2,1)} %param.4, bf16[1,3072,2048]{2,1,0:T(8,128)(2,1)} %param.3), kind=kOutput, calls=%fused_computation.4 | convolution fusion | flops 427917312 | bytes 25821184 | tf_op jit(solution)/shard_map/dot_general | solution.py:20
  171.0 0.0 all-reduce.5.cloned.1.call-update
  171.0 0.0 copy-done
  171.1 0.7 constant_dynamic-slice_fusion
  171.8 69.0 %all-reduce.5.cloned.1.call-done = f32[2048,32]{0,1:T(8,128)} async-done(((f32[2048,32]{0,1:T(8,128)}), f32[2048,32]{0,1:T(8,128)}) %all-reduce.5.cloned.1.call-update) | async-done | bytes 262160 | tf_op jit(solution)/shard_map/psum | solution.py:21
  240.8 1.0 broadcast_multiply_fusion.1
  241.7 0.0 copy-start.1
  241.8 27.5 %fusion.1 = bf16[1,3072,2048]{2,1,0:T(8,128)(2,1)} fusion(f32[32,3072]{1,0:T(8,128)S(1)} %fusion.7, f32[2048,32]{0,1:T(8,128)S(1)} %broadcast_multiply_fusion.1, bf16[1,3072,2048]{2,1,0:T(8,128)(2,1)} %param.4, bf16[1,3072,2048]{2,1,0:T(8,128)(2,1)} %param.3), kind=kOutput, calls=%fused_computation.3 | convolution fusion | flops 2459959296 | bytes 38404096 | tf_op jit(solution)/shard_map/dot_general | solution.py:22
  269.2 0.0 copy-done.1
  (3 shorter events, 0.1 us)
Async XLA Ops:
  7.2 143.2 %all-reduce.3.cloned.1.call-start = ((), (), s32[]{:S(2)}) async-start(), calls=%async_computation | async-start | bytes 786432 | tf_op jit(solution)/shard_map/psum | solution.py:12
  20.0 220.7 %all-reduce.5.cloned.1.call-start = ((), (), s32[]{:S(2)}) async-start(), calls=%async_computation.1 | async-start | bytes 524288 | tf_op jit(solution)/shard_map/psum | solution.py:21
  160.3 10.7 %copy-start = (f32[3072,32]{0,1:T(8,128)S(1)}, f32[3072,32]{0,1:T(8,128)}, u32[]{:S(2)}) copy-start(f32[3072,32]{0,1:T(8,128)} %all-reduce.3.cloned.1.call-done) | copy-start | bytes 1179652
  241.7 27.5 %copy-start.1 = (f32[2048,32]{0,1:T(8,128)}, f32[2048,32]{0,1:T(8,128)S(1)}, u32[]{:S(2)}) copy-start(f32[2048,32]{0,1:T(8,128)S(1)} %broadcast_multiply_fusion.1) | copy-start | bytes 786436
Sparse Core Ops, SparseCore 0:
  20.1 130.2 all-reduce.2
  171.2 69.5 all-reduce.4
where the time goes:
time: 276 us
  waiting for transfers between devices  199 us (72%)
  matrix products  54.1 us (20%)
  between operations  14.1 us (5%)
  other arithmetic  7.69 us (3%)
    psum x1, waiting for transfers between devices, on_device(): left_full = lax.psum(partial_left, ('dp', 'tensor')) / replicas  130 us
    psum x1, waiting for transfers between devices, on_device(): right = lax.psum(local_right, 'dp') / replicas  69 us
    dot_general x1, matrix products, on_device(): approx = jnp.dot(basis, right.T, precision=lax.Precision.HIGHEST)  27.5 us
    dot_general x1, matrix products, on_device(): partial_left = jnp.dot(merged, q_low, preferred_element_type=jnp.float32)  12.8 us
    dot_general x1, matrix products, on_device(): jnp.dot(merged.T, basis_low, preferred_element_type=jnp.float32)  10.7 us
  transfers between devices with their start and end apart: 2, of which 2 were waited for; matrix products, arithmetic and copies ran while one was open for 0% of the time, Pallas kernels for 0%

commit v1 on v0

v1 whole, which is shorter than its diff:
```python
import functools

import jax
import jax.numpy as jnp
from jax import lax
from jax.experimental import pallas as pl
from jax.experimental.pallas import tpu as pltpu
from jax.sharding import PartitionSpec as P

MESH = pl.DeviceIdType.MESH
NT = (((1,), (1,)), ((), ()))
TN = (((0,), (0,)), ((), ()))
BF16, F32 = jnp.bfloat16, jnp.float32
CHUNKS = 3
SLOTS = 4


def split(x):
    high = x.astype(BF16)
    return high, (x - high.astype(F32)).astype(BF16)


def inverse_factor(gram, rank):
    rows = lax.broadcasted_iota(jnp.int32, (rank, 128), 0)
    lanes = lax.broadcasted_iota(jnp.int32, (rank, 128), 1)
    eye = jnp.where(lanes == rows + rank, 1.0, 0.0).astype(F32)
    pad = jnp.concatenate([gram, jnp.zeros((rank, 128 - rank), F32)], axis=1)
    work = pad + eye
    scale = jnp.zeros((rank, 128), F32)
    for j in range(rank):
        row = work[j:j + 1, :]
        pivot = row[:, j:j + 1]
        column = work[:, j:j + 1]
        scale = jnp.where(rows == j, lax.rsqrt(pivot), scale)
        factor = jnp.where(rows[:, :1] > j, column / pivot, 0.0)
        work = work - factor * row
    return (work * scale)[:, rank:2 * rank]


def exchange(T, N, rank, g_hbm, e_hbm, q_ref, merged_ref, left_ref, basis_ref, right_ref,
             gbuf, ebuf, part, s1r, s2s, s2r, full, acc, s5s, s5r, total,
             gsem, esem, s1a, s1b, s2a, s2b, s3a, s3b, s4a, s4b, s5a, s5b, s6a, s6b):
    t, p = lax.axis_index("tensor"), lax.axis_index("dp")
    depth, width = merged_ref.shape
    rows = depth // (CHUNKS * T)
    tiles = CHUNKS * T
    owners, groups, halves = s2s.shape[1], rank // 8, rows // 128
    columns = acc.shape[2]
    blocks = width // columns
    per = N // blocks

    def load(i):
        slot = lax.rem(i, SLOTS)
        where = pl.ds(pl.multiple_of(i * rows, rows), rows)
        return (pltpu.make_async_copy(g_hbm.at[where], gbuf.at[slot], gsem.at[slot]),
                pltpu.make_async_copy(e_hbm.at[where], ebuf.at[slot], esem.at[slot]))

    for i in range(SLOTS):
        for copy in load(i):
            copy.start()

    barrier = pltpu.get_barrier_semaphore()
    for k in range(1, T):
        pl.semaphore_signal(barrier, inc=1, device_id={"tensor": lax.rem(t + k, T)}, device_id_type=MESH)
    for k in range(1, N):
        pl.semaphore_signal(barrier, inc=1, device_id={"dp": lax.rem(p + k, N)}, device_id_type=MESH)
    q_low = q_ref[...].astype(BF16)
    waited = T + N - 2

    def send(src, dst, a, b, axis, peer):
        return pltpu.make_async_remote_copy(
            src_ref=src, dst_ref=dst, send_sem=a, recv_sem=b,
            device_id={axis: peer}, device_id_type=MESH)

    def to_tensor(k):
        return lax.rem(t + k, T)

    def to_dp(k):
        return lax.rem(p + k, N)

    def from_dp(k):
        return lax.rem(p + (N - k), N)

    def when_owner(index, body):
        if owners == N:
            body()
        else:
            pl.when(index < owners)(body)

    def compute(c):
        def tile(i, carry):
            g, e = load(i)
            g.wait()
            e.wait()
            slot = lax.rem(i, SLOTS)
            merged = (gbuf[slot].astype(F32) + ebuf[slot].astype(F32)).astype(BF16)
            merged_ref[pl.ds(pl.multiple_of(i * rows, rows), rows), :] = merged
            part[i] = lax.dot_general(q_low, merged, NT, preferred_element_type=F32)

            @pl.when(i + SLOTS < tiles)
            def _():
                for copy in load(i + SLOTS):
                    copy.start()
            return carry
        lax.fori_loop(c * T, (c + 1) * T, tile, 0)

    def copy1(c, k):
        return send(part.at[c * T + to_tensor(k)], s1r.at[c, k - 1], s1a.at[c, k - 1], s1b.at[c, k - 1], "tensor", to_tensor(k))

    def stage1(c):
        for k in range(1, T):
            copy1(c, k).start()

    def copy2(c, k):
        piece = to_dp(k) if owners == N else jnp.minimum(to_dp(k), owners - 1)
        return send(s2s.at[c, piece], s2r.at[c, k - 1], s2a.at[c, k - 1], s2b.at[c, k - 1], "dp", to_dp(k))

    def stage2(c):
        value = part[c * T + t]
        for k in range(1, T):
            copy1(c, k).wait_recv()
            value = value + s1r[c, k - 1]
        value = value * (1.0 / N)
        for h in range(halves):
            for g in range(groups):
                s2s[c, h * groups + g] = value[g * 8:(g + 1) * 8, h * 128:(h + 1) * 128]
        for k in range(1, N):
            when_owner(to_dp(k), lambda k=k: copy2(c, k).start())

    def copy3(c, k):
        piece = full.at[c, t, p if owners == N else jnp.minimum(p, owners - 1)]
        return send(piece, piece, s3a.at[c, k - 1], s3b.at[c, k - 1], "dp", to_dp(k))

    def stage3(c):
        def body():
            value = s2s[c, p]
            for k in range(1, N):
                copy2(c, k).wait_recv()
                value = value + s2r[c, k - 1]
            full[c, t, p] = value
            for k in range(1, N):
                copy3(c, k).start()
        when_owner(p, body)

    def copy4(c, k):
        return send(full.at[c, t], full.at[c, t], s4a.at[c, k - 1], s4b.at[c, k - 1], "tensor", to_tensor(k))

    def stage4(c):
        for k in range(1, N):
            when_owner(from_dp(k), lambda k=k: copy3(c, k).wait_recv())
        for k in range(1, T):
            copy4(c, k).start()

    def chunk_left(c):
        pieces = []
        for s in range(T):
            for h in range(halves):
                pieces.append(full[c, s, h * groups:(h + 1) * groups].reshape(rank, 128))
        return jnp.concatenate(pieces, axis=1)

    length = T * rows

    def copy5(k):
        return send(s5s.at[to_dp(k)], s5r.at[k - 1], s5a.at[k - 1], s5b.at[k - 1], "dp", to_dp(k))

    def stage5(c):
        for k in range(1, T):
            copy4(c, k).wait_recv()
        left = chunk_left(c)
        left_ref[:, c * length:(c + 1) * length] = left
        both = jnp.concatenate(split(left), axis=0)
        last = c == CHUNKS - 1

        def block(b):
            where = pl.ds(pl.multiple_of(b * columns, columns), columns)
            out = jnp.dot(both, merged_ref[c * length:(c + 1) * length, where], preferred_element_type=F32)
            out = out[:rank] + out[rank:]
            if c > 0:
                out = out + acc[b]
            if not last:
                acc[b] = out
            else:
                high = rank // per
                for i in range(per):
                    s5s[b * per + i] = out[i * high:(i + 1) * high] * (1.0 / N)

        if not last or per > 1:
            def step(b, carry):
                block(b)
                return carry
            lax.fori_loop(0, blocks, step, 0)
            if last:
                for k in range(1, N):
                    copy5(k).start()
        else:
            for k in range(1, N):
                block(to_dp(k))
                copy5(k).start()
            block(p)

    compute(0)
    pl.semaphore_wait(barrier, waited)
    stage1(0)
    compute(1)
    stage1(1)
    stage2(0)
    compute(2)
    stage1(2)
    stage2(1)
    stage3(0)
    stage2(2)
    stage3(1)
    stage4(0)
    stage3(2)
    stage4(1)
    stage5(0)
    stage4(2)
    stage5(1)
    stage5(2)

    left = left_ref[...]
    gram = lax.dot_general(left, left, NT, precision=lax.Precision.HIGHEST, preferred_element_type=F32)
    inverse = inverse_factor(gram, rank)

    def copy6(k):
        return send(total.at[p], total.at[p], s6a.at[k - 1], s6b.at[k - 1], "dp", to_dp(k))

    value = s5s[p]
    for k in range(1, N):
        copy5(k).wait_recv()
        value = value + s5r[k - 1]
    total[p] = value
    for k in range(1, N):
        copy6(k).start()
    basis = jnp.dot(inverse, left, precision=lax.Precision.HIGHEST, preferred_element_type=F32)
    high, low = split(basis)
    basis_ref[...] = jnp.concatenate([high, low, high], axis=0)
    for k in range(1, N):
        copy6(k).wait_recv()
    for b in range(blocks):
        value = jnp.concatenate([total[b * per + i] for i in range(per)], axis=0)
        right_ref[:, b * columns:(b + 1) * columns] = jnp.dot(
            inverse, value, precision=lax.Precision.HIGHEST, preferred_element_type=F32)

    for c in range(CHUNKS):
        for k in range(1, T):
            copy1(c, k).wait_send()
            copy4(c, k).wait_send()
        for k in range(1, N):
            when_owner(to_dp(k), lambda k=k: copy2(c, k).wait_send())
            when_owner(p, lambda k=k: copy3(c, k).wait_send())
    for k in range(1, N):
        copy5(k).wait_send()
        copy6(k).wait_send()


def renew(basis_ref, right_ref, merged_ref, new_ref, out_ref):
    i = pl.program_id(0)
    rows, width = new_ref.shape

    @pl.when(i == 0)
    def _():
        out_ref[...] = right_ref[...]

    start = pl.multiple_of(i * rows, rows)
    step = 512
    basis = basis_ref[...]
    for b in range(width // step):
        cut = slice(b * step, (b + 1) * step)
        high, low = split(right_ref[:, cut])
        factor = jnp.concatenate([high, high, low], axis=0)
        approx = lax.dot_general(basis, factor, TN, preferred_element_type=F32)
        new_ref[:, cut] = (merged_ref[pl.ds(start, rows), cut].astype(F32) - approx).astype(BF16)


def on_device(T, N, grads, errors, q_init):
    depth, width = grads.shape[1:]
    rank = q_init.shape[1]
    rows = depth // (CHUNKS * T)
    owners = (rank // 8) * (rows // 128)
    blocks = min(N, width // 128)
    per = N // blocks
    columns = width // blocks
    piece = (rank // per, columns)
    vmem = pl.BlockSpec(memory_space=pltpu.VMEM)
    hbm = pl.BlockSpec(memory_space=pl.ANY)
    dma = pltpu.SemaphoreType.DMA
    merged, left, basis, right = pl.pallas_call(
        functools.partial(exchange, T, N, rank),
        out_shape=(
            pltpu.VMEM((depth, width), BF16),
            jax.ShapeDtypeStruct((rank, depth), F32),
            jax.ShapeDtypeStruct((3 * rank, depth), BF16),
            jax.ShapeDtypeStruct((rank, width), F32),
        ),
        in_specs=[hbm, hbm, vmem],
        out_specs=(vmem, vmem, vmem, vmem),
        scratch_shapes=[
            pltpu.VMEM((SLOTS, rows, width), BF16),
            pltpu.VMEM((SLOTS, rows, width), BF16),
            pltpu.VMEM((CHUNKS * T, rank, rows), F32),
            pltpu.VMEM((CHUNKS, T - 1, rank, rows), F32),
            pltpu.VMEM((CHUNKS, owners, 8, 128), F32),
            pltpu.VMEM((CHUNKS, N - 1, 8, 128), F32),
            pltpu.VMEM((CHUNKS, T, owners, 8, 128), F32),
            pltpu.VMEM((blocks, rank, columns), F32),
            pltpu.VMEM((N,) + piece, F32),
            pltpu.VMEM((N - 1,) + piece, F32),
            pltpu.VMEM((N,) + piece, F32),
            dma((SLOTS,)), dma((SLOTS,)),
            dma((CHUNKS, T - 1)), dma((CHUNKS, T - 1)),
            dma((CHUNKS, N - 1)), dma((CHUNKS, N - 1)),
            dma((CHUNKS, N - 1)), dma((CHUNKS, N - 1)),
            dma((CHUNKS, T - 1)), dma((CHUNKS, T - 1)),
            dma((N - 1,)), dma((N - 1,)),
            dma((N - 1,)), dma((N - 1,)),
        ],
        compiler_params=pltpu.CompilerParams(
            collective_id=0, has_side_effects=True, vmem_limit_bytes=24 * 2 ** 20),
    )(grads[0], errors[0], q_init.T)

    renew_rows = 256
    renewed, right_out = pl.pallas_call(
        renew,
        grid=(depth // renew_rows,),
        out_shape=(jax.ShapeDtypeStruct((depth, width), BF16), jax.ShapeDtypeStruct((rank, width), F32)),
        in_specs=[
            pl.BlockSpec((3 * rank, renew_rows), lambda i: (0, i)),
            pl.BlockSpec((rank, width), lambda i: (0, 0)),
            vmem,
        ],
        out_specs=(
            pl.BlockSpec((renew_rows, width), lambda i: (i, 0)),
            pl.BlockSpec((rank, width), lambda i: (0, 0)),
        ),
        compiler_params=pltpu.CompilerParams(vmem_limit_bytes=16 * 2 ** 20),
    )(basis, right, merged)

    share = depth // (N * T)
    position = lax.axis_index(("dp", "tensor"))
    left_out = lax.dynamic_slice_in_dim(left, position * share, share, 1).T
    return (left_out, right_out.T, renewed[None])


def solution(mesh):
    return jax.shard_map(
        functools.partial(on_device, mesh.shape["tensor"], mesh.shape["dp"]),
        mesh=mesh,
        in_specs=(P("dp", None, "tensor"), P("dp", None, "tensor"), P("tensor", None)),
        out_specs=(P(("dp", "tensor"), None), P("tensor", None), P("dp", None, "tensor")),
        check_vma=False,
    )
```

time: 276 us -> 58.1 us (0.21)
  waiting for transfers between devices: 199 us -> 0 us
  matrix products: 54.1 us -> 0 us
  Pallas kernels: 0 us -> 51 us
  between operations: 14.1 us -> 0.66 us
  other arithmetic: 7.69 us -> 0 us
  local copies, waits for them, and re-layouts: 0.77 us -> 6.2 us
    psum x2 -> x0, waiting for transfers between devices: 199 us -> none  [the longest x1 130 us: on_device(): left_full = lax.psum(partial_left, ('dp', 'tensor')) / replicas]
    dot_general x4 -> x0, matrix products: 52.5 us -> none  [the longest x1 27.5 us: on_device(): approx = jnp.dot(basis, right.T, precision=lax.Precision.HIGHEST)]
    pallas_call x0 -> x2, Pallas kernels: none -> 51 us  [the longest x1 41.9 us: on_device(): pl.pallas_call(functools.partial(exchange, T, N, rank), out_shape=(pltpu....]
    another operation x5 -> x0, other arithmetic: 6.68 us -> none  [the longest x3 3.6 us: on_device(): lower = jnp.linalg.cholesky(gram)]
    unnamed x4, local copies, waits for them, and re-layouts: 0.01 us -> 5.52 us
  transfers between devices with their start and end apart: 2 -> 0, of which waited for: 2 -> 0; matrix products, arithmetic and copies ran while one was open for 0% -> 0% of each run, Pallas kernels for 0% -> 0%
where the time goes in v1:
time: 58.1 us; the launch traced here: 57.9 us
  Pallas kernels  51 us (88%)
  local copies, waits for them, and re-layouts  6.2 us (11%)
  between operations  0.66 us (1%)
    pallas_call x1, Pallas kernels, on_device(): pl.pallas_call(functools.partial(exchange, T, N, rank), out_shape=(pltpu....  41.9 us
    pallas_call x1, Pallas kernels, on_device(): pl.pallas_call(renew, grid=(depth // renew_rows,), out_shape=(jax.ShapeDt...  9.11 us
    unnamed x4, local copies, waits for them, and re-layouts  5.52 us

profile of v1, /device:TPU:0, one launch (start us, length us, event | category | flops | bytes accessed | tf_op | source)
XLA Modules:
  0.0 57.9 jit_solution(10677969563902094117)
XLA Ops:
  0.6 0.0 copy-start
  0.6 4.6 %copy-done = bf16[1,3072,2048]{2,1,0:T(8,128)(2,1)S(1)} copy-done((bf16[1,3072,2048]{2,1,0:T(8,128)(2,1)S(1)}, bf16[1,3072,2048]{2,1,0:T(8,128)(2,1)}, u32[]{:S(2)}) %copy-start) | copy-done | bytes 12582936
  5.2 0.0 copy-start.1
  5.2 0.9 %copy-done.1 = f32[2048,32]{0,1:T(8,128)S(1)} copy-done((f32[2048,32]{0,1:T(8,128)S(1)}, f32[2048,32]{0,1:T(8,128)}, u32[]{:S(2)}) %copy-start.1) | copy-done | bytes 262168
  6.2 41.9 %shard_map.58 = (bf16[3072,2048]{1,0:T(8,128)(2,1)S(1)}, f32[32,3072]{1,0:T(8,128)S(1)}, bf16[96,3072]{1,0:T(8,128)(2,1)S(1)}, f32[32,2048]{1,0:T(8,128)S(1)}) custom-call(bf16[3072,2048]{1,0:T(8,128)(2,1)S(1)} %bitcast.7, bf16[3072,2048]{1,0:T(8,128)(2,1)} %bitcast.9, f32[32,2048]{1,0:T(8,128)S(1)} %bitcast.8), custom_call_target="tpu_custom_call" | custom-call | tf_op jit(solution)/shard_map/pallas_call | solution.py:288
  48.1 0.7 %dynamic-slice_bitcast_fusion = f32[96,32]{0,1:T(8,128)} fusion(f32[32,3072]{1,0:T(8,128)S(1)} %get-tuple-element.9, s32[]{:T(128)S(6)} %select_n.3), kind=kLoop, calls=%fused_computation | loop fusion | bytes 24580 | tf_op jit(solution)/shard_map/transpose | solution.py:341
  48.8 9.1 %shard_map.59 = (bf16[3072,2048]{1,0:T(8,128)(2,1)}, f32[32,2048]{1,0:T(8,128)}) custom-call(bf16[96,3072]{1,0:T(8,128)(2,1)S(1)} %get-tuple-element.10.basis_ref, f32[32,2048]{1,0:T(8,128)S(1)} %get-tuple-element.11.right_ref, bf16[3072,2048]{1,0:T(8,128)(2,1)S(1)} %get-tuple-element.12.merged_ref), custom_call_target="tpu_custom_call" | custom-call | tf_op jit(solution)/shard_map/pallas_call | solution.py:323
Async XLA Ops:
  0.6 4.6 %copy-start = (bf16[1,3072,2048]{2,1,0:T(8,128)(2,1)S(1)}, bf16[1,3072,2048]{2,1,0:T(8,128)(2,1)}, u32[]{:S(2)}) copy-start(bf16[1,3072,2048]{2,1,0:T(8,128)(2,1)} %param.3) | copy-start | bytes 37748740
  5.2 0.9 %copy-start.1 = (f32[2048,32]{0,1:T(8,128)S(1)}, f32[2048,32]{0,1:T(8,128)}, u32[]{:S(2)}) copy-start(f32[2048,32]{0,1:T(8,128)} %param.5) | copy-start | bytes 786436

commit v2 on v1

--- a/solution.py
+++ b/solution.py
@@ -20,21 +20,25 @@
     return high, (x - high.astype(F32)).astype(BF16)
 
 
-def inverse_factor(gram, rank):
+def eliminate(state, rank, steps):
+    work, scale = state
     rows = lax.broadcasted_iota(jnp.int32, (rank, 128), 0)
-    lanes = lax.broadcasted_iota(jnp.int32, (rank, 128), 1)
-    eye = jnp.where(lanes == rows + rank, 1.0, 0.0).astype(F32)
-    pad = jnp.concatenate([gram, jnp.zeros((rank, 128 - rank), F32)], axis=1)
-    work = pad + eye
-    scale = jnp.zeros((rank, 128), F32)
-    for j in range(rank):
+    for j in steps:
         row = work[j:j + 1, :]
         pivot = row[:, j:j + 1]
         column = work[:, j:j + 1]
         scale = jnp.where(rows == j, lax.rsqrt(pivot), scale)
         factor = jnp.where(rows[:, :1] > j, column / pivot, 0.0)
         work = work - factor * row
-    return (work * scale)[:, rank:2 * rank]
+    return work, scale
+
+
+def augmented(gram, rank):
+    rows = lax.broadcasted_iota(jnp.int32, (rank, 128), 0)
+    lanes = lax.broadcasted_iota(jnp.int32, (rank, 128), 1)
+    eye = jnp.where(lanes == rows + rank, 1.0, 0.0).astype(F32)
+    pad = jnp.concatenate([gram, jnp.zeros((rank, 128 - rank), F32)], axis=1)
+    return pad + eye, jnp.zeros((rank, 128), F32)
 
 
 def exchange(T, N, rank, g_hbm, e_hbm, q_ref, merged_ref, left_ref, basis_ref, right_ref,
@@ -220,7 +224,7 @@
 
     left = left_ref[...]
     gram = lax.dot_general(left, left, NT, precision=lax.Precision.HIGHEST, preferred_element_type=F32)
-    inverse = inverse_factor(gram, rank)
+    state = eliminate(augmented(gram, rank), rank, range(rank // 2))
 
     def copy6(k):
         return send(total.at[p], total.at[p], s6a.at[k - 1], s6b.at[k - 1], "dp", to_dp(k))
@@ -232,9 +236,11 @@
     total[p] = value
     for k in range(1, N):
         copy6(k).start()
+    work, scale = eliminate(state, rank, range(rank // 2, rank))
+    inverse = (work * scale)[:, rank:2 * rank]
     basis = jnp.dot(inverse, left, precision=lax.Precision.HIGHEST, preferred_element_type=F32)
     high, low = split(basis)
-    basis_ref[...] = jnp.concatenate([high, low, high], axis=0)
+    basis_ref[...] = jnp.concatenate([high, low, high], axis=0).T
     for k in range(1, N):
         copy6(k).wait_recv()
     for b in range(blocks):
@@ -254,22 +260,23 @@
         copy6(k).wait_send()
 
 
-def renew(basis_ref, right_ref, merged_ref, new_ref, out_ref):
+def renew(basis_ref, right_ref, merged_ref, new_ref, out_ref, factor_ref):
     i = pl.program_id(0)
     rows, width = new_ref.shape
 
     @pl.when(i == 0)
     def _():
-        out_ref[...] = right_ref[...]
+        right = right_ref[...]
+        out_ref[...] = right
+        high, low = split(right)
+        factor_ref[...] = jnp.concatenate([high, high, low], axis=0)
 
     start = pl.multiple_of(i * rows, rows)
     step = 512
     basis = basis_ref[...]
     for b in range(width // step):
         cut = slice(b * step, (b + 1) * step)
-        high, low = split(right_ref[:, cut])
-        factor = jnp.concatenate([high, high, low], axis=0)
-        approx = lax.dot_general(basis, factor, TN, preferred_element_type=F32)
+        approx = jnp.dot(basis, factor_ref[:, cut], preferred_element_type=F32)
         new_ref[:, cut] = (merged_ref[pl.ds(start, rows), cut].astype(F32) - approx).astype(BF16)
 
 
@@ -290,7 +297,7 @@
         out_shape=(
             pltpu.VMEM((depth, width), BF16),
             jax.ShapeDtypeStruct((rank, depth), F32),
-            jax.ShapeDtypeStruct((3 * rank, depth), BF16),
+            jax.ShapeDtypeStruct((depth, 3 * rank), BF16),
             jax.ShapeDtypeStruct((rank, width), F32),
         ),
         in_specs=[hbm, hbm, vmem],
@@ -316,7 +323,7 @@
             dma((N - 1,)), dma((N - 1,)),
         ],
         compiler_params=pltpu.CompilerParams(
-            collective_id=0, has_side_effects=True, vmem_limit_bytes=24 * 2 ** 20),
+            collective_id=0, has_side_effects=True, vmem_limit_bytes=40 * 2 ** 20),
     )(grads[0], errors[0], q_init.T)
 
     renew_rows = 256
@@ -325,7 +332,7 @@
         grid=(depth // renew_rows,),
         out_shape=(jax.ShapeDtypeStruct((depth, width), BF16), jax.ShapeDtypeStruct((rank, width), F32)),
         in_specs=[
-            pl.BlockSpec((3 * rank, renew_rows), lambda i: (0, i)),
+            pl.BlockSpec((renew_rows, 3 * rank), lambda i: (i, 0)),
             pl.BlockSpec((rank, width), lambda i: (0, 0)),
             vmem,
         ],
@@ -333,6 +340,7 @@
             pl.BlockSpec((renew_rows, width), lambda i: (i, 0)),
             pl.BlockSpec((rank, width), lambda i: (0, 0)),
         ),
+        scratch_shapes=[pltpu.VMEM((3 * rank, width), BF16)],
         compiler_params=pltpu.CompilerParams(vmem_limit_bytes=16 * 2 ** 20),
     )(basis, right, merged)
 

time: 58.1 us -> 55.5 us (0.955)
  local copies, waits for them, and re-layouts: 6.2 us -> 1.63 us
  Pallas kernels: 51 us -> 53 us
    unnamed x4 -> x2, local copies, waits for them, and re-layouts: 5.52 us -> 0.94 us
    pallas_call x1, Pallas kernels: 41.9 us -> 44.2 us  [on_device(): pl.pallas_call(functools.partial(exchange, T, N, rank), out_shape=(pltpu....]
where the time goes in v2:
time: 55.5 us; the launch traced here: 55.3 us
  Pallas kernels  53 us (95%)
  local copies, waits for them, and re-layouts  1.63 us (3%)
  between operations  0.65 us (1%)
    pallas_call x1, Pallas kernels, on_device(): pl.pallas_call(functools.partial(exchange, T, N, rank), out_shape=(pltpu....  44.2 us
    pallas_call x1, Pallas kernels, on_device(): pl.pallas_call(renew, grid=(depth // renew_rows,), out_shape=(jax.ShapeDt...  8.81 us

profile of v2, /device:TPU:0, one launch (start us, length us, event | category | flops | bytes accessed | tf_op | source)
XLA Modules:
  0.0 55.3 jit_solution(12825904036988730704)
XLA Ops:
  0.6 0.0 copy-start
  0.6 0.9 %copy-done = f32[2048,32]{0,1:T(8,128)S(1)} copy-done((f32[2048,32]{0,1:T(8,128)S(1)}, f32[2048,32]{0,1:T(8,128)}, u32[]{:S(2)}) %copy-start) | copy-done | bytes 262168
  1.6 44.2 %shard_map.58 = (bf16[3072,2048]{1,0:T(8,128)(2,1)S(1)}, f32[32,3072]{1,0:T(8,128)S(1)}, bf16[3072,96]{1,0:T(8,128)(2,1)S(1)}, f32[32,2048]{1,0:T(8,128)S(1)}) custom-call(bf16[3072,2048]{1,0:T(8,128)(2,1)} %bitcast.8, bf16[3072,2048]{1,0:T(8,128)(2,1)} %bitcast.9, f32[32,2048]{1,0:T(8,128)S(1)} %bitcast.7), custom_call_target="tpu_custom_call" | custom-call | tf_op jit(solution)/shard_map/pallas_call | solution.py:295
  45.8 0.7 %dynamic-slice_bitcast_fusion = f32[96,32]{0,1:T(8,128)} fusion(f32[32,3072]{1,0:T(8,128)S(1)} %get-tuple-element.9, s32[]{:T(128)S(6)} %select_n.3), kind=kLoop, calls=%fused_computation | loop fusion | bytes 24580 | tf_op jit(solution)/shard_map/transpose | solution.py:349
  46.5 8.8 %shard_map.59 = (bf16[3072,2048]{1,0:T(8,128)(2,1)}, f32[32,2048]{1,0:T(8,128)}) custom-call(bf16[3072,96]{1,0:T(8,128)(2,1)S(1)} %get-tuple-element.10.basis_ref, f32[32,2048]{1,0:T(8,128)S(1)} %get-tuple-element.11.right_ref, bf16[3072,2048]{1,0:T(8,128)(2,1)S(1)} %get-tuple-element.12.merged_ref), custom_call_target="tpu_custom_call" | custom-call | tf_op jit(solution)/shard_map/pallas_call | solution.py:330
Async XLA Ops:
  0.6 1.0 %copy-start = (f32[2048,32]{0,1:T(8,128)S(1)}, f32[2048,32]{0,1:T(8,128)}, u32[]{:S(2)}) copy-start(f32[2048,32]{0,1:T(8,128)} %param.5) | copy-start | bytes 786436
